TPU v7x, 32 devices: a whole 2x2x4 slice. The times are simulated.
32 devices in a mesh: view: 4 (over z), slab: 8 (over y, x, core).
Axes of the slice: x: 2, y: 2, z: 4, core: 2. Of those that a mesh axis runs over, the one named last changes fastest.
Arguments:
- estimate: float32 [256, 32, 128], P('slab'), may hold values from 0.5 to 2
- recorded: float32 [8, 256, 32, 128], P('view', 'slab'), may hold values from 0.5 to 2
- psf_taps: float32 [8, 3, 31], P('view'), may hold values from 0.02 to 1
- tile_map: int32 [8, 8, 8], P('view'), may hold values from 0 to 63, as said below
Outputs:
- new_estimate: float32 [256, 32, 128], P('slab')
Inputs may be any that keep to these rules, and one draw needn't show every extreme that they name: For each view, tile_map[v] is a bijection of the 64 tiles. Each view slab a takes its 8 tiles from the world slabs thus: 2 tiles from world slab a itself, none from exactly one other, one from each of the rest.
All inputs are finite; a program needn't handle non-finite values.
Results may differ from a plain program's by a relative error of at most 0.0003.
Values sent between devices are 32-bit elements; how exact they have to be, the bound alone decides.
A program may use at most 128 MiB of HBM per device.

v0:
```python
import jax
import jax.numpy as jnp
from jax import lax
from jax.sharding import PartitionSpec as P

CAP = 2


exact_mode = lax.Precision.HIGHEST


def padded_2(cells, sides, width):
    for axis, dim in sides:
        count = lax.axis_size(axis)
        ends = count - 1
        head = lax.slice_in_dim(cells, 0, width, axis=dim)
        tail = lax.slice_in_dim(cells, cells.shape[dim] - width, cells.shape[dim], axis=dim)
        cells = jnp.concatenate(
            [
                lax.ppermute(tail, axis, [(i, (i + 1) % count) for i in range(ends)]),
                cells,
                lax.ppermute(head, axis, [((i + 1) % count, i) for i in range(ends)]),
            ],
            axis=dim,
        )
    return cells


def combined_all(value, axis, join):
    pieces = lax.all_gather(value, axis)
    head = pieces[0]
    tail = pieces[1:]
    running, _ = lax.scan(lambda running, share: (join(running, share), None), head, tail)
    return running


def band_forward(weights, length):
    tap_count = weights.shape[1]
    half_width = tap_count // 2
    shape = (tap_count, length, length)
    tap_position = lax.broadcasted_iota(jnp.int32, shape, 0)
    source_position = lax.broadcasted_iota(jnp.int32, shape, 1)
    target_position = lax.broadcasted_iota(jnp.int32, shape, 2)
    hits = (source_position - target_position + half_width == tap_position).astype(jnp.float32)
    kernel = jnp.einsum("vt,tji->vji", weights, hits, precision=exact_mode)
    divisor = jnp.sum(kernel, axis=1)
    return kernel / divisor[:, None, :]


def depth_band(weights, depth_rows, adjoint):
    tap_count = weights.shape[1]
    half_width = tap_count // 2
    shape = (tap_count, depth_rows + 2 * half_width, depth_rows)
    tap_position = lax.broadcasted_iota(jnp.int32, shape, 0)
    padded_position = lax.broadcasted_iota(jnp.int32, shape, 1)
    target_position = lax.broadcasted_iota(jnp.int32, shape, 2)
    if adjoint:
        hits = target_position + 2 * half_width - padded_position == tap_position
    else:
        hits = padded_position - target_position == tap_position
    return jnp.einsum("vt,tki->vki", weights, hits.astype(jnp.float32), precision=exact_mode)


def depth_divisor(weights, depth_rows, own_slab, total_rows):
    tap_count = weights.shape[1]
    half_width = tap_count // 2
    row_numbers = own_slab * depth_rows + jnp.arange(depth_rows, dtype=jnp.int32)
    shifted = row_numbers[None, :] + jnp.arange(tap_count, dtype=jnp.int32)[:, None] - half_width
    inside = ((shifted >= 0) & (shifted < total_rows)).astype(jnp.float32)
    return jnp.einsum("vt,ti->vi", weights, inside, precision=exact_mode)


def pick_rows(arrays, indices):
    return jax.vmap(lambda table, chosen: table[chosen])(arrays, indices)


def multiply(first, second):
    return first * second


def local(estimate, recorded, psf_taps, tile_map):
    view_count = psf_taps.shape[0]
    tap_count = psf_taps.shape[2]
    half_width = tap_count // 2
    depth_rows, height_rows, width_rows = estimate.shape
    grid_size = lax.axis_size("slab")
    tile_rows = height_rows // grid_size
    own_slab = lax.axis_index("slab")
    weights = psf_taps / jnp.sum(psf_taps, axis=-1, keepdims=True)
    source_slab = tile_map // grid_size
    source_tile = tile_map % grid_size
    slab_range = jnp.arange(grid_size, dtype=jnp.int32)
    slot_range = jnp.arange(CAP, dtype=jnp.int32)
    same_source = (source_slab[..., None] == slab_range).astype(jnp.int32)
    earlier = jnp.cumsum(same_source, axis=2) - same_source
    slot_rank = jnp.sum(earlier * same_source, axis=3)
    own_source = lax.dynamic_index_in_dim(source_slab, own_slab, 1, keepdims=False)
    own_rank = lax.dynamic_index_in_dim(slot_rank, own_slab, 1, keepdims=False)
    world_tiles = estimate.reshape(depth_rows, grid_size, tile_rows, width_rows).transpose(
        1, 0, 2, 3
    )
    outgoing = (source_slab[:, :, None, :] == own_slab) & (
        slot_rank[:, :, None, :] == slot_range[None, None, :, None]
    )
    outgoing_count = outgoing.astype(jnp.int32)
    picked_tile = jnp.sum(outgoing_count * source_tile[:, :, None, :], axis=3)
    filled = jnp.sum(outgoing_count, axis=3).astype(jnp.float32)
    sending = world_tiles[picked_tile] * filled[..., None, None, None]
    arrived = lax.all_to_all(sending, "slab", split_axis=1, concat_axis=1, tiled=True)
    arrived_flat = arrived.reshape(view_count, grid_size * CAP, depth_rows, tile_rows, width_rows)
    view_tiles = pick_rows(arrived_flat, own_source * CAP + own_rank)
    viewed = view_tiles.transpose(0, 2, 1, 3, 4).reshape(
        view_count, depth_rows, height_rows, width_rows
    )
    total_rows = depth_rows * grid_size
    divisor = depth_divisor(weights[:, 0], depth_rows, own_slab, total_rows)
    height_band = band_forward(weights[:, 1], height_rows)
    width_band = band_forward(weights[:, 2], width_rows)
    padded = padded_2(viewed, (("slab", 1),), half_width)
    blurred = jnp.einsum(
        "vkyx,vki->viyx", padded, depth_band(weights[:, 0], depth_rows, False), precision=exact_mode
    )
    blurred = blurred / divisor[:, :, None, None]
    blurred = jnp.einsum("vzyx,vyk->vzkx", blurred, height_band, precision=exact_mode)
    blurred = jnp.einsum("vzyx,vxk->vzyk", blurred, width_band, precision=exact_mode)
    scaled = recorded / blurred / divisor[:, :, None, None]
    padded_ratio = padded_2(scaled, (("slab", 1),), half_width)
    adjoint_volume = jnp.einsum(
        "vkyx,vki->viyx",
        padded_ratio,
        depth_band(weights[:, 0], depth_rows, True),
        precision=exact_mode,
    )
    adjoint_volume = jnp.einsum("vzyx,vky->vzkx", adjoint_volume, height_band, precision=exact_mode)
    adjoint_volume = jnp.einsum("vzyx,vkx->vzyk", adjoint_volume, width_band, precision=exact_mode)
    back_tiles = adjoint_volume.reshape(
        view_count, depth_rows, grid_size, tile_rows, width_rows
    ).transpose(0, 2, 1, 3, 4)
    target_tiles = own_slab * grid_size + slab_range
    matches = (tile_map[:, None, :, :] == target_tiles[None, :, None, None]).astype(jnp.int32)
    from_slab = jnp.sum(matches * slab_range[None, None, :, None], axis=(2, 3))
    from_rank = jnp.sum(matches * slot_rank[:, None, :, :], axis=(2, 3))
    first_back = (
        (own_source[:, None, :] == slab_range[None, :, None]) & (own_rank[:, None, :] == 0)
    ).astype(jnp.int32)
    chosen_first = jnp.sum(first_back * slab_range[None, None, :], axis=2)
    used_first = jnp.sum(first_back, axis=2).astype(jnp.float32)
    sending_back = pick_rows(back_tiles, chosen_first) * used_first[..., None, None, None]
    returned = lax.all_to_all(sending_back, "slab", split_axis=1, concat_axis=1, tiled=True)
    second_index = jnp.sum((own_rank == 1).astype(jnp.int32) * slab_range[None, :], axis=1)
    kept_tile = pick_rows(back_tiles, second_index[:, None])
    remote_back = pick_rows(returned, from_slab)
    world_back = jnp.where((from_rank == 1)[..., None, None, None], kept_tile, remote_back)
    correction = world_back.transpose(0, 2, 1, 3, 4).reshape(
        view_count, depth_rows, height_rows, width_rows
    )
    local_product = jnp.prod(correction, axis=0)
    total_product = combined_all(local_product, "view", multiply)
    return estimate * total_product


def solution(mesh):
    in_specs = (
        P("slab", None, None),
        P("view", "slab", None, None),
        P("view", None, None),
        P("view", None, None),
    )
    out_specs = P("slab", None, None)
    return jax.shard_map(local, mesh=mesh, in_specs=in_specs, out_specs=out_specs, check_vma=False)
```

profile of v0, /device:TPU:0, one launch (start us, length us, event | category | flops | bytes accessed | tf_op | source)
XLA Modules:
  0.0 167.8 jit_solution(8009698657775351527)
XLA Ops:
  6.5 0.7 add_select_fusion
  7.2 0.7 broadcast_compare_fusion
  9.0 1.4 copy.76
  10.4 0.7 gather_fusion
  11.3 1.6 copy.79
  12.9 5.3 %all-to-all-start = ((f32[2,8,2,32,4,128]{5,3,4,2,0,1:T(8,128)}), f32[2,8,2,32,4,128]{5,3,4,2,0,1:T(8,128)S(1)}, u32[]{:S(2)}, u32[]{:S(2)}) async-start(f32[2,8,2,32,4,128]{5,3,4,2,0,1:T(8,128)} %copy.79), calls=%async_computation | async-start | bytes 4194304 | tf_op jit(solution)/shard_map/all_to_all | solution.py:109
  19.2 25.6 %all-to-all-done = f32[2,8,2,32,4,128]{5,3,4,2,0,1:T(8,128)S(1)} async-done(((f32[2,8,2,32,4,128]{5,3,4,2,0,1:T(8,128)}), f32[2,8,2,32,4,128]{5,3,4,2,0,1:T(8,128)S(1)}, u32[]{:S(2)}, u32[]{:S(2)}) %all-to-all-start) | async-done | bytes 2097184 | tf_op jit(solution)/shard_map/all_to_all | solution.py:109
  44.8 1.6 copy.80
  46.4 2.2 %gather_fusion.1 = f32[16,32,4,128]{3,1,2,0:T(8,128)S(1)} fusion(f32[2,16,32,4,128]{4,2,3,1,0:T(8,128)} %bitcast.91, s32[16]{0:T(128)S(1)} %reshape.145), kind=kCustom, calls=%fused_computation.1 | custom fusion | bytes 2097280 | tf_op jit(solution)/shard_map/vmap()/gather | solution.py:74
  48.7 1.3 collective-permute-start
  50.0 1.3 collective-permute-start.1
  51.5 0.8 fusion.73
  52.3 2.2 %collective-permute-done.1 = f32[2,15,32,128]{3,1,2,0:T(8,128)S(1)} collective-permute-done((f32[2,15,32,128]{3,1,2,0:T(8,128)S(1)}, f32[2,15,32,128]{3,1,2,0:T(8,128)S(1)}, u32[]{:S(2)}, u32[]{:S(2)}) %collective-permute-start.1) | collective-permute-done | bytes 491552 | tf_op jit(solution)/shard_map/ppermute | solution.py:22
  54.5 1.3 fusion.14
  55.8 1.6 convolution_bitcast_fusion.1
  57.4 2.5 %fusion.13 = f32[2,32,32,128]{3,1,2,0:T(8,128)S(1)} fusion(f32[2,32,32,128]{3,2,1,0:T(8,128)S(1)} %convolution_bitcast_fusion.1, f32[2,32,32,128]{3,2,1,0:T(8,128)S(1)} %copy-done.3, f32[2,32]{1,0:T(2,128)S(1)} %fusion.38, f32[2,128,128,1]{2,0,1,3:T(2,128)S(1)} %divide_bitcast_fusion), kind=kOutput, calls=%fused_computation.22 | convolution fusion | flops 403177472 | bytes 3277056 | tf_op jit(solution)/shard_map/vzyx,vxk->vzyk/dot_general | solution.py:125
  60.0 12.0 %collective-permute-start.2 = (f32[2,15,32,128]{3,1,2,0:T(8,128)S(1)}, f32[2,15,32,128]{3,1,2,0:T(8,128)S(1)}, u32[]{:S(2)}, u32[]{:S(2)}) collective-permute-start(f32[2,15,32,128]{3,1,2,0:T(8,128)S(1)} %get-tuple-element.39), channel_id=1, source_target_pairs={{0,1},{1,2},{2,3},{3,4},{4,5},{5,6},{6,7},{8,9},{9,10},{10,11},{11... | collective-permute-start | bytes 1474568 | tf_op jit(solution)/shard_map/ppermute | solution.py:20
  72.0 1.5 collective-permute-start.3
  73.6 0.7 fusion.27
  74.7 1.1 collective-permute-done.3
  75.8 1.3 fusion.6
  77.1 1.6 convolution_bitcast_fusion
  78.7 1.0 fusion.24
  81.1 1.7 %copy.94 = f32[2,8,32,4,128]{4,3,2,0,1:T(4,128)} copy(f32[2,8,32,4,128]{4,2,3,1,0:T(8,128)S(1)} %broadcast_multiply_fusion.1) | data formatting | bytes 2097152 | tf_op jit(solution)/shard_map/mul | solution.py:148
  82.8 9.9 %all-to-all-start.1 = ((f32[2,8,32,4,128]{4,3,2,0,1:T(4,128)}), f32[2,8,32,4,128]{4,3,2,0,1:T(4,128)S(1)}, u32[]{:S(2)}, u32[]{:S(2)}) async-start(f32[2,8,32,4,128]{4,3,2,0,1:T(4,128)} %copy.94), calls=%async_computation.1 | async-start | bytes 2097152 | tf_op jit(solution)/shard_map/all_to_all | solution.py:149
  94.0 14.2 %all-to-all-done.1 = f32[2,8,32,4,128]{4,3,2,0,1:T(4,128)S(1)} async-done(((f32[2,8,32,4,128]{4,3,2,0,1:T(4,128)}), f32[2,8,32,4,128]{4,3,2,0,1:T(4,128)S(1)}, u32[]{:S(2)}, u32[]{:S(2)}) %all-to-all-start.1) | async-done | bytes 1048608 | tf_op jit(solution)/shard_map/all_to_all | solution.py:149
  108.2 1.2 gather_fusion.4
  109.8 1.1 copy.96
  110.9 45.5 %all-gather.2.cloned.1.call-done = f32[4,32,32,128]{3,2,1,0:T(8,128)} async-done(((f32[1,32,32,128]{3,2,1,0:T(8,128)}), f32[4,32,32,128]{3,2,1,0:T(8,128)}) %all-gather.2.cloned.1.call-update) | async-done | bytes 2097168 | tf_op jit(solution)/shard_map/all_gather | solution.py:30
  156.4 1.5 slice.56
  158.0 1.1 slice_bitcast_fusion
  160.1 0.9 mul.100
  (65 shorter events, 7.6 us)
Async XLA Ops:
  12.9 5.4 %copy-start.2 = (f32[2,3,31]{2,0,1:T(2,128)S(1)}, f32[2,3,31]{2,0,1:T(2,128)}, u32[]{:S(2)}) copy-start(f32[2,3,31]{2,0,1:T(2,128)} %param.8) | copy-start | bytes 2236
  12.9 31.9 %all-to-all-start = ((f32[2,8,2,32,4,128]{5,3,4,2,0,1:T(8,128)}), f32[2,8,2,32,4,128]{5,3,4,2,0,1:T(8,128)S(1)}, u32[]{:S(2)}, u32[]{:S(2)}) async-start(f32[2,8,2,32,4,128]{5,3,4,2,0,1:T(8,128)} %copy.79), calls=%async_computation | async-start | bytes 4194304 | tf_op jit(solution)/shard_map/all_to_all | solution.py:109
  48.7 3.6 %collective-permute-start = (f32[2,15,32,128]{3,1,2,0:T(8,128)S(1)}, f32[2,15,32,128]{3,1,2,0:T(8,128)S(1)}, u32[]{:S(2)}, u32[]{:S(2)}) collective-permute-start(f32[2,15,32,128]{3,1,2,0:T(8,128)S(1)} %get-tuple-element.41), channel_id=1, source_target_pairs={{0,1},{1,2},{2,3},{3,4},{4,5},{5,6},{6,7},{8,9},{9,10},{10,11},{11... | collective-permute-start | bytes 1474568 | tf_op jit(solution)/shard_map/ppermute | solution.py:20
  50.0 4.5 %collective-permute-start.1 = (f32[2,15,32,128]{3,1,2,0:T(8,128)S(1)}, f32[2,15,32,128]{3,1,2,0:T(8,128)S(1)}, u32[]{:S(2)}, u32[]{:S(2)}) collective-permute-start(f32[2,15,32,128]{3,1,2,0:T(8,128)S(1)} %get-tuple-element.42), channel_id=1, source_target_pairs={{1,0},{2,1},{3,2},{4,3},{5,4},{6,5},{7,6},{9,8},{10,9},{11,10},{12... | collective-permute-start | bytes 1474568 | tf_op jit(solution)/shard_map/ppermute | solution.py:22
  55.8 1.6 copy-start.3
  59.9 13.7 %copy-start.1 = (s32[2,8,8]{2,1,0:T(8,128)S(1)}, s32[2,8,8]{2,1,0:T(8,128)}, u32[]{:S(2)}) copy-start(s32[2,8,8]{2,1,0:T(8,128)} %param.9) | copy-start | bytes 1540
  60.0 14.7 %collective-permute-start.2 = (f32[2,15,32,128]{3,1,2,0:T(8,128)S(1)}, f32[2,15,32,128]{3,1,2,0:T(8,128)S(1)}, u32[]{:S(2)}, u32[]{:S(2)}) collective-permute-start(f32[2,15,32,128]{3,1,2,0:T(8,128)S(1)} %get-tuple-element.39), channel_id=1, source_target_pairs={{0,1},{1,2},{2,3},{3,4},{4,5},{5,6},{6,7},{8,9},{9,10},{10,11},{11... | collective-permute-start | bytes 1474568 | tf_op jit(solution)/shard_map/ppermute | solution.py:20
  72.0 3.8 %collective-permute-start.3 = (f32[2,15,32,128]{3,1,2,0:T(8,128)S(1)}, f32[2,15,32,128]{3,1,2,0:T(8,128)S(1)}, u32[]{:S(2)}, u32[]{:S(2)}) collective-permute-start(f32[2,15,32,128]{3,1,2,0:T(8,128)S(1)} %get-tuple-element.40), channel_id=1, source_target_pairs={{1,0},{2,1},{3,2},{4,3},{5,4},{6,5},{7,6},{9,8},{10,9},{11,10},{12... | collective-permute-start | bytes 1474568 | tf_op jit(solution)/shard_map/ppermute | solution.py:22
  82.8 25.3 %all-to-all-start.1 = ((f32[2,8,32,4,128]{4,3,2,0,1:T(4,128)}), f32[2,8,32,4,128]{4,3,2,0,1:T(4,128)S(1)}, u32[]{:S(2)}, u32[]{:S(2)}) async-start(f32[2,8,32,4,128]{4,3,2,0,1:T(4,128)} %copy.94), calls=%async_computation.1 | async-start | bytes 2097152 | tf_op jit(solution)/shard_map/all_to_all | solution.py:149
  92.7 63.7 %all-gather.2.cloned.1.call-start = ((), (), s32[]{:S(2)}) async-start(), calls=%async_computation.2 | async-start | bytes 2621440 | tf_op jit(solution)/shard_map/all_gather | solution.py:30
  159.0 1.0 copy-start
Sparse Core Ops, SparseCore 0:
  111.0 45.3 all-gather.1
where the time goes:
time: 168 us
  waiting for transfers between devices  88.6 us (53%)
  starting transfers between devices  31.4 us (19%)
  local copies, waits for them, and re-layouts  17.2 us (10%)
  between operations  13.8 us (8%)
  matrix products  11 us (7%)
  other arithmetic  5.72 us (3%)
    all_gather x1, waiting for transfers between devices, combined_all(): pieces = lax.all_gather(value, axis)  45.5 us
    all_to_all x1, waiting for transfers between devices, local(): lax.all_to_all(sending, 'slab', split_axis=1, concat_axis=1, tiled=True)  25.6 us
    all_to_all x1, waiting for transfers between devices, local(): lax.all_to_all(sending_back, 'slab', split_axis=1, concat_axis=1, tiled=T...  14.2 us
    ppermute x2, starting transfers between devices, padded_2(): lax.ppermute(tail, axis, [(i, (i + 1) % count) for i in range(ends)])  13.3 us
    all_to_all x1, starting transfers between devices, local(): lax.all_to_all(sending_back, 'slab', split_axis=1, concat_axis=1, tiled=T...  9.93 us
    all_to_all x1, starting transfers between devices, local(): lax.all_to_all(sending, 'slab', split_axis=1, concat_axis=1, tiled=True)  5.3 us
    gather x9, local copies, waits for them, and re-layouts, pick_rows(): return jax.vmap(lambda table, chosen: table[chosen])(arrays, indices)  4.98 us
  transfers between devices with their start and end apart: 7, of which 5 were waited for; matrix products, arithmetic and copies ran while one was open for 3% of the time, Pallas kernels for 0%

commit v1 on v0

v1 whole, which is shorter than its diff:
```python
import functools

import jax
import jax.numpy as jnp
from jax import lax
from jax.experimental import pallas as pl
from jax.experimental.pallas import tpu as pltpu
from jax.sharding import PartitionSpec as P

HALO = 16
MESH = pl.DeviceIdType.MESH
F32 = jnp.float32
BF16 = jnp.bfloat16


def split(value):
    high = value.astype(BF16)
    low = (value - high.astype(F32)).astype(BF16)
    return high, low


def stacked(value, axis):
    high, low = split(value)
    return jnp.concatenate([high, low, high], axis=axis)


def dot(left, right):
    return jnp.dot(left, right, preferred_element_type=F32)


def select_taps(position, tap, taps):
    total = jnp.zeros(position.shape, F32)
    for t in range(taps):
        total = jnp.where(position == t, tap(t), total)
    return total


def column_divisor(columns, tap, taps, length):
    half = taps // 2
    total = jnp.zeros(columns.shape, F32)
    for t in range(taps):
        cell = columns + (t - half)
        total = total + jnp.where((cell >= 0) & (cell < length), tap(t), 0.0)
    return total


def kernel(n, m, views, taps, *refs):
    table, tap_ref, est_ref, rec_ref, out_ref = refs[:5]
    rest = list(refs[5:])
    height, depth, width = rec_ref.shape[2], rec_ref.shape[1], rec_ref.shape[3]
    tile = height // n
    padded = depth + 2 * HALO
    half = taps // 2
    view = lax.axis_index("view")
    own = lax.axis_index("slab")
    est_t = rest.pop(0)
    send = rest.pop(0)
    arrived = [rest.pop(0) for _ in range(views)]
    pad1 = [rest.pop(0) for _ in range(views)]
    pad2 = [rest.pop(0) for _ in range(views)]
    work = [rest.pop(0) for _ in range(views)]
    back = [[rest.pop(0) for _ in range(tile)] for _ in range(views)]
    up_in, up_out, down_in, down_out = [rest.pop(0) for _ in range(4)]
    lz, lza, ly, lya, rx, rxa = [rest.pop(0) for _ in range(6)]
    f_send, f_recv, h_send, h_recv, b_send, b_recv, c_send, c_recv = rest

    barrier = pltpu.get_barrier_semaphore()

    for v in range(views):
        for pad in (pad1[v], pad2[v]):
            pad[:, 0:HALO, :] = jnp.zeros((height, HALO, width), F32)
            pad[:, HALO + depth:, :] = jnp.zeros((height, HALO, width), F32)

    for r in range(1, n):
        pl.semaphore_signal(barrier, inc=1, device_id=(view, lax.rem(own + r, n)), device_id_type=MESH)
    for r in range(1, m):
        pl.semaphore_signal(barrier, inc=1, device_id=(lax.rem(view + r, m), own), device_id_type=MESH)

    for g in range(height // 8):
        block = jnp.swapaxes(est_ref[:, g * 8:g * 8 + 8, :], 0, 1)
        if tile <= 8:
            per = 8 // tile
            est_t[g * per:(g + 1) * per] = block.reshape(per, tile, depth, width)

    pl.semaphore_wait(barrier, n - 1 + m - 1)

    def forward_copy(v, r):
        return pltpu.make_async_remote_copy(
            src_ref=send.at[v, r], dst_ref=arrived[v].at[r],
            send_sem=f_send.at[v, r], recv_sem=f_recv.at[v, r],
            device_id=(view, lax.rem(own + r, n)), device_id_type=MESH)

    for v in range(views):
        for r in range(1, n):
            send[v, r] = est_t[table[v, 0, r]]
            forward_copy(v, r).start()

    for v in range(views):
        for axis in range(3):
            tap = lambda t, v=v, axis=axis: tap_ref[v, axis, t]
            if axis < 2:
                rows, cols, shift, length, start = (
                    (depth, padded, HALO, depth * n, own * depth) if axis == 0 else (height, height, 0, height, 0))
                shape = (rows, 3 * cols)
                row = start + lax.broadcasted_iota(jnp.int32, shape, 0)
                flat = lax.broadcasted_iota(jnp.int32, shape, 1)
                group = (flat >= cols).astype(jnp.int32) + (flat >= 2 * cols).astype(jnp.int32)
                col = start + flat - group * cols - shift
                inside = (col >= 0) & (col < length)
                f = jnp.where(inside, select_taps(col - row + half, tap, taps), 0.0)
                f = f / jnp.sum(jnp.where(group == 0, f, 0.0), axis=1, keepdims=True)
                div = column_divisor(col[0:8], tap, taps, length)[0:1]
                a = jnp.where(inside, select_taps(row - col + half, tap, taps), 0.0)
                a = a / jnp.where(inside[0:1], div, 1.0)
                for ref, value in (((lz, lza), (ly, lya))[axis][0], f), (((lz, lza), (ly, lya))[axis][1], a):
                    high, low = split(value)
                    ref[v] = jnp.where(group == 2, low.astype(F32), high.astype(F32)).astype(BF16)
            else:
                shape = (width, width)
                row = lax.broadcasted_iota(jnp.int32, shape, 0)
                col = lax.broadcasted_iota(jnp.int32, shape, 1)
                f = select_taps(col - row + half, tap, taps)
                f = f / jnp.sum(f, axis=1, keepdims=True)
                a = select_taps(row - col + half, tap, taps)
                a = a / column_divisor(col[0:8], tap, taps, width)[0:1]
                for ref, value in ((rx, a), (rxa, f)):
                    high, low = split(value)
                    ref[v, 0:width] = high
                    ref[v, width:2 * width] = high
                    ref[v, 2 * width:] = low

    has_low, has_high = own > 0, own < n - 1

    def halo_copies(pads, stage, v):
        low = pltpu.make_async_remote_copy(
            src_ref=pads[v].at[:, HALO:2 * HALO, :], dst_ref=pads[v].at[:, HALO + depth:2 * HALO + depth, :],
            send_sem=h_send.at[stage, v, 0], recv_sem=h_recv.at[stage, v, 0],
            device_id=(view, lax.rem(own + n - 1, n)), device_id_type=MESH)
        high = pltpu.make_async_remote_copy(
            src_ref=pads[v].at[:, depth:depth + HALO, :], dst_ref=pads[v].at[:, 0:HALO, :],
            send_sem=h_send.at[stage, v, 1], recv_sem=h_recv.at[stage, v, 1],
            device_id=(view, lax.rem(own + 1, n)), device_id_type=MESH)
        return low, high

    def halo_start(pads, stage, v):
        low, high = halo_copies(pads, stage, v)

        @pl.when(has_low)
        def _():
            low.start()

        @pl.when(has_high)
        def _():
            high.start()

    def halo_wait(pads, stage, v):
        low, high = halo_copies(pads, stage, v)

        @pl.when(has_low)
        def _():
            low.wait_send()
            high.wait_recv()

        @pl.when(has_high)
        def _():
            high.wait_send()
            low.wait_recv()

    def assemble(v):
        for r in range(1, n):
            forward_copy(v, r).wait()
        for c in range(n):
            slot = table[v, 1, c]
            value = jnp.where(slot == 0, est_t[table[v, 2, c]], arrived[v][slot])
            pad1[v][c * tile:(c + 1) * tile, HALO:HALO + depth, :] = value
        halo_start(pad1, 0, v)

    def blur_and_ratio(v):
        halo_wait(pad1, 0, v)

        def first(g, carry):
            left, right = lz[v], rx[v]
            rows = [dot(left, stacked(pad1[v][g * 4 + k], 0)) for k in range(4)]
            value = dot(stacked(jnp.concatenate(rows, axis=0), 1), right)
            work[v][pl.ds(g * 4, 4)] = value.reshape(4, depth, width)
            return carry

        lax.fori_loop(0, height // 4, first, 0)

        def second(g, carry):
            base = pl.multiple_of(g * 8, 8)
            left, left_a, right = ly[v], lya[v], rxa[v]
            block = jnp.swapaxes(work[v][:, pl.ds(base, 8), :], 0, 1)
            rows = []
            for k in range(8):
                blurred = dot(left, stacked(block[k], 0))
                ratio = rec_ref[v, base + k] / blurred
                rows.append(dot(left_a, stacked(ratio, 0)))
            value = dot(stacked(jnp.concatenate(rows, axis=0), 1), right)
            value = jnp.swapaxes(value.reshape(8, height, width), 0, 1)
            pad2[v][:, pl.ds(pl.multiple_of(base + HALO, 8), 8), :] = value
            return carry

        lax.fori_loop(0, depth // 8, second, 0)
        halo_start(pad2, 1, v)

    def back_copy(v, r, q):
        return pltpu.make_async_remote_copy(
            src_ref=send.at[v, r, q], dst_ref=back[v][q].at[r],
            send_sem=b_send.at[v, r, q], recv_sem=b_recv.at[v, r, q],
            device_id=(view, lax.rem(own + r, n)), device_id_type=MESH)

    def finish(v):
        halo_wait(pad2, 1, v)
        for q in range(tile):
            def last(c, carry):
                work[v][c * tile + q] = dot(lza[v], stacked(pad2[v][c * tile + q], 0))
                return carry

            lax.fori_loop(0, n, last, 0, unroll=4)
            for r in range(1, n):
                send[v, r, q] = work[v][table[v, 3, r] * tile + q]
                back_copy(v, r, q).start()

    for v in range(views):
        assemble(v)
    for v in range(views):
        blur_and_ratio(v)
    for v in range(views):
        finish(v)

    has_below, has_above = view > 0, view < m - 1

    def up_copy(q):
        return pltpu.make_async_remote_copy(
            src_ref=up_out.at[q], dst_ref=up_in.at[q], send_sem=c_send.at[0, q], recv_sem=c_recv.at[0, q],
            device_id=(lax.rem(view + 1, m), own), device_id_type=MESH)

    def down_copy(q):
        return pltpu.make_async_remote_copy(
            src_ref=down_out.at[q], dst_ref=down_in.at[q], send_sem=c_send.at[1, q], recv_sem=c_recv.at[1, q],
            device_id=(lax.rem(view + m - 1, m), own), device_id_type=MESH)

    def local_product(q):
        for v in range(views):
            for r in range(1, n):
                back_copy(v, r, q).wait()
        for k in range(n):
            product = None
            for v in range(views):
                slot = table[v, 4, k]
                value = jnp.where(slot == 0, work[v][table[v, 5, k] * tile + q], back[v][q][slot])
                product = value if product is None else product * value
            out_ref[q, k] = product

        @pl.when(view == 0)
        def _():
            up_out[q] = out_ref[q]
            up_copy(q).start()

        @pl.when(view == m - 1)
        def _():
            down_out[q] = out_ref[q]
            down_copy(q).start()

    def relay(q):
        @pl.when(has_below & has_above)
        def _():
            up_copy(q).wait_recv()
            up_out[q] = up_in[q] * out_ref[q]
            up_copy(q).start()
            down_copy(q).wait_recv()
            down_out[q] = down_in[q] * out_ref[q]
            down_copy(q).start()
            out_ref[q] = up_out[q] * down_in[q]

        @pl.when(has_below & jnp.logical_not(has_above))
        def _():
            up_copy(q).wait_recv()
            out_ref[q] = up_in[q] * out_ref[q]

        @pl.when(has_above & jnp.logical_not(has_below))
        def _():
            down_copy(q).wait_recv()
            out_ref[q] = out_ref[q] * down_in[q]

    for q in range(tile):
        local_product(q)
        if q > 0:
            relay(q - 1)
    relay(tile - 1)
    for q in range(tile):
        @pl.when(has_above)
        def _():
            up_copy(q).wait_send()

        @pl.when(has_below)
        def _():
            down_copy(q).wait_send()


def local(n, m, estimate, recorded, psf_taps, tile_map):
    views, _, taps = psf_taps.shape
    depth, height, width = estimate.shape
    tile = height // n
    own = lax.axis_index("slab")
    count = jnp.arange(n, dtype=jnp.int32)
    flat = tile_map.reshape(views, 1, n * n)
    where_shown = (flat == (own * n + count)[None, :, None]).astype(jnp.int32)
    inverse = jnp.sum(where_shown * jnp.arange(n * n, dtype=jnp.int32), axis=2)
    shown = lax.dynamic_index_in_dim(tile_map, own, 1, keepdims=False)

    def choose(slabs):
        ahead = (slabs - own + n) % n
        hits = (ahead[:, None, :] == count[None, :, None]) & (count[None, :, None] > 0)
        return jnp.sum(hits.astype(jnp.int32) * count, axis=2)

    table = jnp.stack(
        [choose(inverse // n), (own - shown // n + n) % n, shown % n,
         choose(shown // n), (own - inverse // n + n) % n, inverse % n], axis=1)

    padded = depth + 2 * HALO
    vmem = pltpu.VMEM
    dma = pltpu.SemaphoreType.DMA
    scratch = [vmem((n, tile, depth, width), F32), vmem((views, n, tile, depth, width), F32)]
    scratch += [vmem((n, tile, depth, width), F32) for _ in range(views)]
    scratch += [vmem((height, padded, width), F32) for _ in range(2 * views)]
    scratch += [vmem((height, depth, width), F32) for _ in range(views)]
    scratch += [vmem((n, depth, width), F32) for _ in range(views * tile)]
    scratch += [vmem((tile, n, depth, width), F32) for _ in range(4)]
    scratch += [vmem((views, depth, 3 * padded), BF16) for _ in range(2)]
    scratch += [vmem((views, height, 3 * height), BF16) for _ in range(2)]
    scratch += [vmem((views, 3 * width, width), BF16) for _ in range(2)]
    scratch += [dma((views, n)), dma((views, n)), dma((2, views, 2)), dma((2, views, 2)),
                dma((views, n, tile)), dma((views, n, tile)), dma((2, tile)), dma((2, tile))]
    product = pl.pallas_call(
        functools.partial(kernel, n, m, views, taps),
        out_shape=jax.ShapeDtypeStruct((tile, n, depth, width), F32),
        in_specs=[pl.BlockSpec(memory_space=pltpu.SMEM)] * 2 + [pl.BlockSpec(memory_space=pltpu.VMEM)] * 2,
        out_specs=pl.BlockSpec(memory_space=pltpu.VMEM),
        scratch_shapes=scratch,
        compiler_params=pltpu.CompilerParams(
            collective_id=0, has_side_effects=True, vmem_limit_bytes=60 * 1024 * 1024),
    )(table, psf_taps, estimate, recorded)
    return estimate * product.transpose(2, 1, 0, 3).reshape(depth, height, width)


def solution(mesh):
    n, m = mesh.shape["slab"], mesh.shape["view"]
    in_specs = (
        P("slab", None, None),
        P("view", "slab", None, None),
        P("view", None, None),
        P("view", None, None),
    )
    return jax.shard_map(
        functools.partial(local, n, m), mesh=mesh, in_specs=in_specs,
        out_specs=P("slab", None, None), check_vma=False)
```

time: 168 us -> 101 us (0.60)
  Pallas kernels: 0 us -> 96 us
  waiting for transfers between devices: 88.6 us -> 0 us
  starting transfers between devices: 31.4 us -> 0 us
  between operations: 13.8 us -> 0.06 us
  local copies, waits for them, and re-layouts: 17.2 us -> 4.33 us
  matrix products: 11 us -> 0 us
  other arithmetic: 5.72 us -> 0.81 us
    pallas_call x0 -> x1, Pallas kernels: none -> 96 us  [local(): pl.pallas_call(functools.partial(kernel, n, m, views, taps), out_shape=ja...]
    all_gather x1 -> x0, waiting for transfers between devices: 45.5 us -> none  [combined_all(): pieces = lax.all_gather(value, axis)]
    all_to_all x2 -> x0, waiting for transfers between devices: 39.8 us -> none  [the longest x1 25.6 us: local(): lax.all_to_all(sending, 'slab', split_axis=1, concat_axis=1, tiled=True)]
    ppermute x4 -> x0, starting transfers between devices: 16.1 us -> none  [the longest x2 13.3 us: padded_2(): lax.ppermute(tail, axis, [(i, (i + 1) % count) for i in range(ends)])]
    all_to_all x2 -> x0, starting transfers between devices: 15.2 us -> none  [the longest x1 9.93 us: local(): lax.all_to_all(sending_back, 'slab', split_axis=1, concat_axis=1, tiled=T...]
    dot_general x11 -> x0, matrix products: 11 us -> none  [the longest x1 2.47 us: local(): jnp.einsum('vzyx,vxk->vzyk', blurred, width_band, precision=exact_mode)]
    gather x10 -> x0, local copies, waits for them, and re-layouts: 5.67 us -> none  [the longest x9 4.98 us: pick_rows(): return jax.vmap(lambda table, chosen: table[chosen])(arrays, indices)]
    ppermute x4 -> x0, waiting for transfers between devices: 3.34 us -> none  [the longest x2 3.33 us: padded_2(): lax.ppermute(head, axis, [((i + 1) % count, i) for i in range(ends)])]
  transfers between devices with their start and end apart: 7 -> 0, of which waited for: 5 -> 0; matrix products, arithmetic and copies ran while one was open for 3% -> 0% of each run, Pallas kernels for 0% -> 0%
where the time goes in v1:
time: 101 us
  Pallas kernels  96 us (95%)
  local copies, waits for them, and re-layouts  4.33 us (4%)
    pallas_call x1, Pallas kernels, local(): pl.pallas_call(functools.partial(kernel, n, m, views, taps), out_shape=ja...  96 us

profile of v1, /device:TPU:0, one launch (start us, length us, event | category | flops | bytes accessed | tf_op | source)
XLA Modules:
  0.0 101.2 jit_solution(6494636653013160041)
XLA Ops:
  0.0 0.0 copy-start.1
  0.0 0.7 copy-done.1
  0.7 0.1 eq.50
  0.8 0.2 select_reduce_fusion.2
  1.1 0.2 select_reduce_fusion
  1.3 0.0 copy-start.2
  1.3 0.6 stack.15.refs_0_
  1.9 0.1 copy-done.2
  2.0 0.6 copy.28.refs_1_
  2.6 96.0 %shard_map.46 = f32[4,8,32,128]{3,2,1,0:T(8,128)} custom-call(s32[2,6,8]{2,1,0:T(8,128)} %stack.15.refs_0_, f32[2,3,31]{2,1,0:T(4,128)} %copy.28.refs_1_, f32[32,32,128]{2,1,0:T(8,128)} %refs_2_.1, f32[2,32,32,128]{3,2,1,0:T(8,128)} %refs_3_.1), custom_call_target="tpu_custom_call" | custom-call | tf_op jit(solution)/shard_map/pallas_call | solution.py:336
  98.5 0.0 copy-start
  98.6 1.1 %copy.29 = f32[32,8,4,128]{3,0,2,1:T(8,128)S(1)} copy(f32[32,8,4,128]{3,0,1,2:T(8,128)} %bitcast.13) | data formatting | bytes 1048576 | tf_op jit(solution)/shard_map/transpose | solution.py:345
  99.7 0.0 copy-done
  99.7 0.3 bitcast_multiply_fusion
  100.1 1.1 %copy.31 = f32[32,32,128]{2,1,0:T(8,128)} copy(f32[32,32,128]{2,0,1:T(8,128)S(1)} %bitcast_multiply_fusion) | data formatting | bytes 1048576 | tf_op jit(solution)/shard_map/mul | solution.py:345
  (6 shorter events, 0.1 us)
Async XLA Ops:
  0.0 0.7 copy-start.1
  1.3 0.7 copy-start.2
  98.5 1.2 %copy-start = (f32[32,32,128]{2,1,0:T(8,128)S(1)}, f32[32,32,128]{2,1,0:T(8,128)}, u32[]{:S(2)}) copy-start(f32[32,32,128]{2,1,0:T(8,128)} %refs_2_.1) | copy-start | bytes 1572868

commit v2 on v1

--- a/solution.py
+++ b/solution.py
@@ -8,6 +8,7 @@
 from jax.sharding import PartitionSpec as P
 
 HALO = 16
+PARTS = 1
 MESH = pl.DeviceIdType.MESH
 F32 = jnp.float32
 BF16 = jnp.bfloat16
@@ -230,73 +231,112 @@
         finish(v)
 
     has_below, has_above = view > 0, view < m - 1
-
-    def up_copy(q):
+    lower = 2 * view < m
+    parts = up_in.shape[0] // tile
+    share = n // parts
+    chunks = tile * parts
+
+    def up_copy(i):
         return pltpu.make_async_remote_copy(
-            src_ref=up_out.at[q], dst_ref=up_in.at[q], send_sem=c_send.at[0, q], recv_sem=c_recv.at[0, q],
+            src_ref=up_out.at[i], dst_ref=up_in.at[i], send_sem=c_send.at[0, i], recv_sem=c_recv.at[0, i],
             device_id=(lax.rem(view + 1, m), own), device_id_type=MESH)
 
-    def down_copy(q):
+    def down_copy(i):
         return pltpu.make_async_remote_copy(
-            src_ref=down_out.at[q], dst_ref=down_in.at[q], send_sem=c_send.at[1, q], recv_sem=c_recv.at[1, q],
+            src_ref=down_out.at[i], dst_ref=down_in.at[i], send_sem=c_send.at[1, i], recv_sem=c_recv.at[1, i],
             device_id=(lax.rem(view + m - 1, m), own), device_id_type=MESH)
 
-    def local_product(q):
-        for v in range(views):
-            for r in range(1, n):
-                back_copy(v, r, q).wait()
-        for k in range(n):
+    def local_product(i):
+        q, part = i // parts, i % parts
+        if part == 0:
+            for v in range(views):
+                for r in range(1, n):
+                    back_copy(v, r, q).wait()
+        for k in range(share):
             product = None
             for v in range(views):
-                slot = table[v, 4, k]
-                value = jnp.where(slot == 0, work[v][table[v, 5, k] * tile + q], back[v][q][slot])
+                world = part * share + k
+                slot = table[v, 4, world]
+                value = jnp.where(slot == 0, work[v][table[v, 5, world] * tile + q], back[v][q][slot])
                 product = value if product is None else product * value
-            out_ref[q, k] = product
+            out_ref[i, k] = product
 
         @pl.when(view == 0)
         def _():
-            up_out[q] = out_ref[q]
-            up_copy(q).start()
+            up_out[i] = out_ref[i]
+            up_copy(i).start()
 
         @pl.when(view == m - 1)
         def _():
-            down_out[q] = out_ref[q]
-            down_copy(q).start()
-
-    def relay(q):
+            down_out[i] = out_ref[i]
+            down_copy(i).start()
+
+    def pass_up(i):
+        @pl.when(has_below)
+        def _():
+            up_copy(i).wait_recv()
+
+            @pl.when(has_above)
+            def _():
+                up_out[i] = up_in[i] * out_ref[i]
+                up_copy(i).start()
+
+    def pass_down(i):
+        @pl.when(has_above)
+        def _():
+            down_copy(i).wait_recv()
+
+            @pl.when(has_below)
+            def _():
+                down_out[i] = down_in[i] * out_ref[i]
+                down_copy(i).start()
+
+    def near(i):
+        @pl.when(lower)
+        def _():
+            pass_up(i)
+
+        @pl.when(jnp.logical_not(lower))
+        def _():
+            pass_down(i)
+
+    def far(i):
+        @pl.when(lower)
+        def _():
+            pass_down(i)
+
+        @pl.when(jnp.logical_not(lower))
+        def _():
+            pass_up(i)
+
         @pl.when(has_below & has_above)
         def _():
-            up_copy(q).wait_recv()
-            up_out[q] = up_in[q] * out_ref[q]
-            up_copy(q).start()
-            down_copy(q).wait_recv()
-            down_out[q] = down_in[q] * out_ref[q]
-            down_copy(q).start()
-            out_ref[q] = up_out[q] * down_in[q]
+            out_ref[i] = up_out[i] * down_in[i]
 
         @pl.when(has_below & jnp.logical_not(has_above))
         def _():
-            up_copy(q).wait_recv()
-            out_ref[q] = up_in[q] * out_ref[q]
+            out_ref[i] = out_ref[i] * up_in[i]
 
         @pl.when(has_above & jnp.logical_not(has_below))
         def _():
-            down_copy(q).wait_recv()
-            out_ref[q] = out_ref[q] * down_in[q]
-
-    for q in range(tile):
-        local_product(q)
-        if q > 0:
-            relay(q - 1)
-    relay(tile - 1)
-    for q in range(tile):
+            out_ref[i] = out_ref[i] * down_in[i]
+
+    for i in range(chunks):
+        local_product(i)
+        if i >= parts:
+            near(i - parts)
+    for i in range(chunks - parts, chunks):
+        near(i)
+    for i in range(chunks):
+        far(i)
+    for i in range(chunks):
         @pl.when(has_above)
-        def _():
-            up_copy(q).wait_send()
+        def _(i=i):
+            up_copy(i).wait_send()
 
         @pl.when(has_below)
-        def _():
-            down_copy(q).wait_send()
+        def _(i=i):
+            down_copy(i).wait_send()
 
 
 def local(n, m, estimate, recorded, psf_taps, tile_map):
@@ -327,21 +367,24 @@
     scratch += [vmem((height, padded, width), F32) for _ in range(2 * views)]
     scratch += [vmem((height, depth, width), F32) for _ in range(views)]
     scratch += [vmem((n, depth, width), F32) for _ in range(views * tile)]
-    scratch += [vmem((tile, n, depth, width), F32) for _ in range(4)]
+    parts = PARTS if n % PARTS == 0 else 1
+    chunks = tile * parts
+    scratch += [vmem((chunks, n // parts, depth, width), F32) for _ in range(4)]
     scratch += [vmem((views, depth, 3 * padded), BF16) for _ in range(2)]
     scratch += [vmem((views, height, 3 * height), BF16) for _ in range(2)]
     scratch += [vmem((views, 3 * width, width), BF16) for _ in range(2)]
     scratch += [dma((views, n)), dma((views, n)), dma((2, views, 2)), dma((2, views, 2)),
-                dma((views, n, tile)), dma((views, n, tile)), dma((2, tile)), dma((2, tile))]
+                dma((views, n, tile)), dma((views, n, tile)), dma((2, chunks)), dma((2, chunks))]
     product = pl.pallas_call(
         functools.partial(kernel, n, m, views, taps),
-        out_shape=jax.ShapeDtypeStruct((tile, n, depth, width), F32),
+        out_shape=jax.ShapeDtypeStruct((chunks, n // parts, depth, width), F32),
         in_specs=[pl.BlockSpec(memory_space=pltpu.SMEM)] * 2 + [pl.BlockSpec(memory_space=pltpu.VMEM)] * 2,
         out_specs=pl.BlockSpec(memory_space=pltpu.VMEM),
         scratch_shapes=scratch,
         compiler_params=pltpu.CompilerParams(
             collective_id=0, has_side_effects=True, vmem_limit_bytes=60 * 1024 * 1024),
     )(table, psf_taps, estimate, recorded)
+    product = product.reshape(tile, n, depth, width)
     return estimate * product.transpose(2, 1, 0, 3).reshape(depth, height, width)
 
 

time: 101 us -> 86 us (0.85)
  Pallas kernels: 96 us -> 80.5 us
    pallas_call x1, Pallas kernels: 96 us -> 80.5 us  [local(): pl.pallas_call(functools.partial(kernel, n, m, views, taps), out_shape=ja...]
where the time goes in v2:
time: 86 us; the launch traced here: 85.7 us
  Pallas kernels  80.5 us (94%)
  local copies, waits for them, and re-layouts  4.33 us (5%)
    pallas_call x1, Pallas kernels, local(): pl.pallas_call(functools.partial(kernel, n, m, views, taps), out_shape=ja...  80.5 us

profile of v2, /device:TPU:0, one launch (start us, length us, event | category | flops | bytes accessed | tf_op | source)
XLA Modules:
  0.0 85.7 jit_solution(5417082244041302135)
XLA Ops:
  0.0 0.0 copy-start.1
  0.0 0.7 copy-done.1
  0.7 0.1 eq.50
  0.8 0.2 select_reduce_fusion.2
  1.1 0.2 select_reduce_fusion
  1.3 0.0 copy-start.2
  1.3 0.6 stack.15.refs_0_
  1.9 0.1 copy-done.2
  2.0 0.6 copy.28.refs_1_
  2.6 80.5 %shard_map.46 = f32[4,8,32,128]{3,2,1,0:T(8,128)} custom-call(s32[2,6,8]{2,1,0:T(8,128)} %stack.15.refs_0_, f32[2,3,31]{2,1,0:T(4,128)} %copy.28.refs_1_, f32[32,32,128]{2,1,0:T(8,128)} %refs_2_.1, f32[2,32,32,128]{3,2,1,0:T(8,128)} %refs_3_.1), custom_call_target="tpu_custom_call" | custom-call | tf_op jit(solution)/shard_map/pallas_call | solution.py:378
  83.1 0.0 copy-start
  83.1 1.1 %copy.29 = f32[32,8,4,128]{3,0,2,1:T(8,128)S(1)} copy(f32[32,8,4,128]{3,0,1,2:T(8,128)} %bitcast.13) | data formatting | bytes 1048576 | tf_op jit(solution)/shard_map/transpose | solution.py:388
  84.3 0.0 copy-done
  84.3 0.3 bitcast_multiply_fusion
  84.6 1.1 %copy.31 = f32[32,32,128]{2,1,0:T(8,128)} copy(f32[32,32,128]{2,0,1:T(8,128)S(1)} %bitcast_multiply_fusion) | data formatting | bytes 1048576 | tf_op jit(solution)/shard_map/mul | solution.py:388
  (6 shorter events, 0.1 us)
Async XLA Ops:
  0.0 0.7 copy-start.1
  1.3 0.7 copy-start.2
  83.1 1.2 %copy-start = (f32[32,32,128]{2,1,0:T(8,128)S(1)}, f32[32,32,128]{2,1,0:T(8,128)}, u32[]{:S(2)}) copy-start(f32[32,32,128]{2,1,0:T(8,128)} %refs_2_.1) | copy-start | bytes 1572868

commit v3 on v2

--- a/solution.py
+++ b/solution.py
@@ -68,9 +68,10 @@
     barrier = pltpu.get_barrier_semaphore()
 
     for v in range(views):
-        for pad in (pad1[v], pad2[v]):
-            pad[:, 0:HALO, :] = jnp.zeros((height, HALO, width), F32)
-            pad[:, HALO + depth:, :] = jnp.zeros((height, HALO, width), F32)
+        pad1[v][:, 0:HALO, :] = jnp.zeros((height, HALO, width), F32)
+        pad1[v][:, HALO + depth:, :] = jnp.zeros((height, HALO, width), F32)
+        pad2[v][:, :, 0:HALO, :] = jnp.zeros((n, tile, HALO, width), F32)
+        pad2[v][:, :, HALO + depth:, :] = jnp.zeros((n, tile, HALO, width), F32)
 
     for r in range(1, n):
         pl.semaphore_signal(barrier, inc=1, device_id=(view, lax.rem(own + r, n)), device_id_type=MESH)
@@ -132,19 +133,27 @@
 
     has_low, has_high = own > 0, own < n - 1
 
-    def halo_copies(pads, stage, v):
+    def halo_copies(v, q):
+        if q is None:
+            pad, slot = pad1[v], tile
+            own_low, own_high = pad.at[:, HALO:2 * HALO, :], pad.at[:, depth:depth + HALO, :]
+            far_high, far_low = pad.at[:, HALO + depth:2 * HALO + depth, :], pad.at[:, 0:HALO, :]
+        else:
+            pad, slot = pad2[v], q
+            own_low, own_high = pad.at[:, q, HALO:2 * HALO, :], pad.at[:, q, depth:depth + HALO, :]
+            far_high, far_low = pad.at[:, q, HALO + depth:2 * HALO + depth, :], pad.at[:, q, 0:HALO, :]
         low = pltpu.make_async_remote_copy(
-            src_ref=pads[v].at[:, HALO:2 * HALO, :], dst_ref=pads[v].at[:, HALO + depth:2 * HALO + depth, :],
-            send_sem=h_send.at[stage, v, 0], recv_sem=h_recv.at[stage, v, 0],
+            src_ref=own_low, dst_ref=far_high,
+            send_sem=h_send.at[v, slot, 0], recv_sem=h_recv.at[v, slot, 0],
             device_id=(view, lax.rem(own + n - 1, n)), device_id_type=MESH)
         high = pltpu.make_async_remote_copy(
-            src_ref=pads[v].at[:, depth:depth + HALO, :], dst_ref=pads[v].at[:, 0:HALO, :],
-            send_sem=h_send.at[stage, v, 1], recv_sem=h_recv.at[stage, v, 1],
+            src_ref=own_high, dst_ref=far_low,
+            send_sem=h_send.at[v, slot, 1], recv_sem=h_recv.at[v, slot, 1],
             device_id=(view, lax.rem(own + 1, n)), device_id_type=MESH)
         return low, high
 
-    def halo_start(pads, stage, v):
-        low, high = halo_copies(pads, stage, v)
+    def halo_start(v, q=None):
+        low, high = halo_copies(v, q)
 
         @pl.when(has_low)
         def _():
@@ -154,8 +163,8 @@
         def _():
             high.start()
 
-    def halo_wait(pads, stage, v):
-        low, high = halo_copies(pads, stage, v)
+    def halo_wait(v, q=None):
+        low, high = halo_copies(v, q)
 
         @pl.when(has_low)
         def _():
@@ -174,10 +183,10 @@
             slot = table[v, 1, c]
             value = jnp.where(slot == 0, est_t[table[v, 2, c]], arrived[v][slot])
             pad1[v][c * tile:(c + 1) * tile, HALO:HALO + depth, :] = value
-        halo_start(pad1, 0, v)
+        halo_start(v)
 
     def blur_and_ratio(v):
-        halo_wait(pad1, 0, v)
+        halo_wait(v)
 
         def first(g, carry):
             left, right = lz[v], rx[v]
@@ -198,12 +207,13 @@
                 ratio = rec_ref[v, base + k] / blurred
                 rows.append(dot(left_a, stacked(ratio, 0)))
             value = dot(stacked(jnp.concatenate(rows, axis=0), 1), right)
-            value = jnp.swapaxes(value.reshape(8, height, width), 0, 1)
-            pad2[v][:, pl.ds(pl.multiple_of(base + HALO, 8), 8), :] = value
+            value = jnp.swapaxes(value.reshape(8, height, width), 0, 1).reshape(n, tile, 8, width)
+            pad2[v][:, :, pl.ds(pl.multiple_of(base + HALO, 8), 8), :] = value
             return carry
 
         lax.fori_loop(0, depth // 8, second, 0)
-        halo_start(pad2, 1, v)
+        for q in range(tile):
+            halo_start(v, q)
 
     def back_copy(v, r, q):
         return pltpu.make_async_remote_copy(
@@ -211,25 +221,22 @@
             send_sem=b_send.at[v, r, q], recv_sem=b_recv.at[v, r, q],
             device_id=(view, lax.rem(own + r, n)), device_id_type=MESH)
 
-    def finish(v):
-        halo_wait(pad2, 1, v)
-        for q in range(tile):
-            def last(c, carry):
-                work[v][c * tile + q] = dot(lza[v], stacked(pad2[v][c * tile + q], 0))
-                return carry
-
-            lax.fori_loop(0, n, last, 0, unroll=4)
-            for r in range(1, n):
-                send[v, r, q] = work[v][table[v, 3, r] * tile + q]
-                back_copy(v, r, q).start()
+    def finish(v, q):
+        halo_wait(v, q)
+
+        def last(c, carry):
+            work[v][c * tile + q] = dot(lza[v], stacked(pad2[v][c, q], 0))
+            return carry
+
+        lax.fori_loop(0, n, last, 0, unroll=4)
+        for r in range(1, n):
+            send[v, r, q] = work[v][table[v, 3, r] * tile + q]
+            back_copy(v, r, q).start()
 
     for v in range(views):
         assemble(v)
     for v in range(views):
         blur_and_ratio(v)
-    for v in range(views):
-        finish(v)
-
     has_below, has_above = view > 0, view < m - 1
     lower = 2 * view < m
     parts = up_in.shape[0] // tile
@@ -321,8 +328,15 @@
         def _():
             out_ref[i] = out_ref[i] * down_in[i]
 
+    ahead = min(2, tile)
+    for q in range(ahead):
+        for v in range(views):
+            finish(v, q)
     for i in range(chunks):
         local_product(i)
+        if i % parts == 0 and i // parts + ahead < tile:
+            for v in range(views):
+                finish(v, i // parts + ahead)
         if i >= parts:
             near(i - parts)
     for i in range(chunks - parts, chunks):
@@ -364,7 +378,8 @@
     dma = pltpu.SemaphoreType.DMA
     scratch = [vmem((n, tile, depth, width), F32), vmem((views, n, tile, depth, width), F32)]
     scratch += [vmem((n, tile, depth, width), F32) for _ in range(views)]
-    scratch += [vmem((height, padded, width), F32) for _ in range(2 * views)]
+    scratch += [vmem((height, padded, width), F32) for _ in range(views)]
+    scratch += [vmem((n, tile, padded, width), F32) for _ in range(views)]
     scratch += [vmem((height, depth, width), F32) for _ in range(views)]
     scratch += [vmem((n, depth, width), F32) for _ in range(views * tile)]
     parts = PARTS if n % PARTS == 0 else 1
@@ -373,7 +388,7 @@
     scratch += [vmem((views, depth, 3 * padded), BF16) for _ in range(2)]
     scratch += [vmem((views, height, 3 * height), BF16) for _ in range(2)]
     scratch += [vmem((views, 3 * width, width), BF16) for _ in range(2)]
-    scratch += [dma((views, n)), dma((views, n)), dma((2, views, 2)), dma((2, views, 2)),
+    scratch += [dma((views, n)), dma((views, n)), dma((views, tile + 1, 2)), dma((views, tile + 1, 2)),
                 dma((views, n, tile)), dma((views, n, tile)), dma((2, chunks)), dma((2, chunks))]
     product = pl.pallas_call(
         functools.partial(kernel, n, m, views, taps),

time: 86 us -> 82 us (0.953)
  Pallas kernels: 80.5 us -> 76.5 us
    pallas_call x1, Pallas kernels: 80.5 us -> 76.5 us  [local(): pl.pallas_call(functools.partial(kernel, n, m, views, taps), out_shape=ja...]
where the time goes in v3:
time: 82 us; the launch traced here: 81.7 us
  Pallas kernels  76.5 us (93%)
  local copies, waits for them, and re-layouts  4.33 us (5%)
    pallas_call x1, Pallas kernels, local(): pl.pallas_call(functools.partial(kernel, n, m, views, taps), out_shape=ja...  76.5 us

profile of v3, /device:TPU:0, one launch (start us, length us, event | category | flops | bytes accessed | tf_op | source)
XLA Modules:
  0.0 81.7 jit_solution(14933928325710215892)
XLA Ops:
  0.0 0.0 copy-start.1
  0.0 0.7 copy-done.1
  0.7 0.1 eq.50
  0.8 0.2 select_reduce_fusion.2
  1.1 0.2 select_reduce_fusion
  1.3 0.0 copy-start.2
  1.3 0.6 stack.15.refs_0_
  1.9 0.1 copy-done.2
  2.0 0.6 copy.28.refs_1_
  2.6 76.5 %shard_map.46 = f32[4,8,32,128]{3,2,1,0:T(8,128)} custom-call(s32[2,6,8]{2,1,0:T(8,128)} %stack.15.refs_0_, f32[2,3,31]{2,1,0:T(4,128)} %copy.28.refs_1_, f32[32,32,128]{2,1,0:T(8,128)} %refs_2_.1, f32[2,32,32,128]{3,2,1,0:T(8,128)} %refs_3_.1), custom_call_target="tpu_custom_call" | custom-call | tf_op jit(solution)/shard_map/pallas_call | solution.py:393
  79.1 0.0 copy-start
  79.1 1.1 %copy.29 = f32[32,8,4,128]{3,0,2,1:T(8,128)S(1)} copy(f32[32,8,4,128]{3,0,1,2:T(8,128)} %bitcast.13) | data formatting | bytes 1048576 | tf_op jit(solution)/shard_map/transpose | solution.py:403
  80.3 0.0 copy-done
  80.3 0.3 bitcast_multiply_fusion
  80.6 1.1 %copy.31 = f32[32,32,128]{2,1,0:T(8,128)} copy(f32[32,32,128]{2,0,1:T(8,128)S(1)} %bitcast_multiply_fusion) | data formatting | bytes 1048576 | tf_op jit(solution)/shard_map/mul | solution.py:403
  (6 shorter events, 0.1 us)
Async XLA Ops:
  0.0 0.7 copy-start.1
  1.3 0.7 copy-start.2
  79.1 1.2 %copy-start = (f32[32,32,128]{2,1,0:T(8,128)S(1)}, f32[32,32,128]{2,1,0:T(8,128)}, u32[]{:S(2)}) copy-start(f32[32,32,128]{2,1,0:T(8,128)} %refs_2_.1) | copy-start | bytes 1572868

commit v4 on v3

--- a/solution.py
+++ b/solution.py
@@ -46,7 +46,7 @@
 
 
 def kernel(n, m, views, taps, *refs):
-    table, tap_ref, est_ref, rec_ref, out_ref = refs[:5]
+    map_ref, tap_ref, est_ref, rec_ref, out_ref = refs[:5]
     rest = list(refs[5:])
     height, depth, width = rec_ref.shape[2], rec_ref.shape[1], rec_ref.shape[3]
     tile = height // n
@@ -63,7 +63,7 @@
     back = [[rest.pop(0) for _ in range(tile)] for _ in range(views)]
     up_in, up_out, down_in, down_out = [rest.pop(0) for _ in range(4)]
     lz, lza, ly, lya, rx, rxa = [rest.pop(0) for _ in range(6)]
-    f_send, f_recv, h_send, h_recv, b_send, b_recv, c_send, c_recv = rest
+    f_send, f_recv, h_send, h_recv, b_send, b_recv, c_send, c_recv, table = rest
 
     barrier = pltpu.get_barrier_semaphore()
 
@@ -92,10 +92,59 @@
             send_sem=f_send.at[v, r], recv_sem=f_recv.at[v, r],
             device_id=(view, lax.rem(own + r, n)), device_id_type=MESH)
 
+    step = min(8, n)
+
+    def slab_of(world):
+        return lax.div(world, jnp.int32(n))
+
+    def bounded(index):
+        return jnp.minimum(jnp.maximum(index, 0), n - 1)
+
+    for v in range(views):
+        def pick(r, carry, v=v):
+            peer = lax.rem(own + r, n)
+
+            def add(c, total):
+                world = map_ref[v, peer, c]
+                slab = slab_of(world)
+                return total + jnp.where(slab == own, world - slab * n, 0)
+
+            table[v, 0, r] = bounded(lax.fori_loop(0, n, add, jnp.int32(0), unroll=step))
+            return carry
+
+        lax.fori_loop(0, n, pick, 0)
+
     for v in range(views):
         for r in range(1, n):
-            send[v, r] = est_t[table[v, 0, r]]
+            send[v, r] = est_t[bounded(table[v, 0, r])]
             forward_copy(v, r).start()
+
+    for v in range(views):
+        def fill(k, carry, v=v):
+            world = map_ref[v, own, k]
+            slab = slab_of(world)
+            table[v, 1, k] = bounded(lax.rem(own - slab + n, n))
+            table[v, 2, k] = bounded(world - slab * n)
+            peer = lax.rem(own + k, n)
+
+            def back_tile(c, total):
+                return total + jnp.where(slab_of(map_ref[v, own, c]) == peer, c, 0)
+
+            table[v, 3, k] = bounded(lax.fori_loop(0, n, back_tile, jnp.int32(0), unroll=step))
+
+            def scan_slab(a, total):
+                def scan_tile(c, total):
+                    return total + jnp.where(map_ref[v, a, c] == own * n + k, a * n + c, 0)
+
+                return lax.fori_loop(0, n, scan_tile, total, unroll=step)
+
+            shown = lax.fori_loop(0, n, scan_slab, jnp.int32(0))
+            slab = slab_of(shown)
+            table[v, 4, k] = bounded(lax.rem(own - slab + n, n))
+            table[v, 5, k] = bounded(shown - slab * n)
+            return carry
+
+        lax.fori_loop(0, n, fill, 0)
 
     for v in range(views):
         for axis in range(3):
@@ -180,8 +229,8 @@
         for r in range(1, n):
             forward_copy(v, r).wait()
         for c in range(n):
-            slot = table[v, 1, c]
-            value = jnp.where(slot == 0, est_t[table[v, 2, c]], arrived[v][slot])
+            slot = bounded(table[v, 1, c])
+            value = jnp.where(slot == 0, est_t[bounded(table[v, 2, c])], arrived[v][slot])
             pad1[v][c * tile:(c + 1) * tile, HALO:HALO + depth, :] = value
         halo_start(v)
 
@@ -230,7 +279,7 @@
 
         lax.fori_loop(0, n, last, 0, unroll=4)
         for r in range(1, n):
-            send[v, r, q] = work[v][table[v, 3, r] * tile + q]
+            send[v, r, q] = work[v][bounded(table[v, 3, r]) * tile + q]
             back_copy(v, r, q).start()
 
     for v in range(views):
@@ -263,8 +312,8 @@
             product = None
             for v in range(views):
                 world = part * share + k
-                slot = table[v, 4, world]
-                value = jnp.where(slot == 0, work[v][table[v, 5, world] * tile + q], back[v][q][slot])
+                slot = bounded(table[v, 4, world])
+                value = jnp.where(slot == 0, work[v][bounded(table[v, 5, world]) * tile + q], back[v][q][slot])
                 product = value if product is None else product * value
             out_ref[i, k] = product
 
@@ -357,22 +406,6 @@
     views, _, taps = psf_taps.shape
     depth, height, width = estimate.shape
     tile = height // n
-    own = lax.axis_index("slab")
-    count = jnp.arange(n, dtype=jnp.int32)
-    flat = tile_map.reshape(views, 1, n * n)
-    where_shown = (flat == (own * n + count)[None, :, None]).astype(jnp.int32)
-    inverse = jnp.sum(where_shown * jnp.arange(n * n, dtype=jnp.int32), axis=2)
-    shown = lax.dynamic_index_in_dim(tile_map, own, 1, keepdims=False)
-
-    def choose(slabs):
-        ahead = (slabs - own + n) % n
-        hits = (ahead[:, None, :] == count[None, :, None]) & (count[None, :, None] > 0)
-        return jnp.sum(hits.astype(jnp.int32) * count, axis=2)
-
-    table = jnp.stack(
-        [choose(inverse // n), (own - shown // n + n) % n, shown % n,
-         choose(shown // n), (own - inverse // n + n) % n, inverse % n], axis=1)
-
     padded = depth + 2 * HALO
     vmem = pltpu.VMEM
     dma = pltpu.SemaphoreType.DMA
@@ -389,7 +422,7 @@
     scratch += [vmem((views, height, 3 * height), BF16) for _ in range(2)]
     scratch += [vmem((views, 3 * width, width), BF16) for _ in range(2)]
     scratch += [dma((views, n)), dma((views, n)), dma((views, tile + 1, 2)), dma((views, tile + 1, 2)),
-                dma((views, n, tile)), dma((views, n, tile)), dma((2, chunks)), dma((2, chunks))]
+                dma((views, n, tile)), dma((views, n, tile)), dma((2, chunks)), dma((2, chunks)), pltpu.SMEM((views, 6, n), jnp.int32)]
     product = pl.pallas_call(
         functools.partial(kernel, n, m, views, taps),
         out_shape=jax.ShapeDtypeStruct((chunks, n // parts, depth, width), F32),
@@ -398,7 +431,7 @@
         scratch_shapes=scratch,
         compiler_params=pltpu.CompilerParams(
             collective_id=0, has_side_effects=True, vmem_limit_bytes=60 * 1024 * 1024),
-    )(table, psf_taps, estimate, recorded)
+    )(tile_map, psf_taps, estimate, recorded)
     product = product.reshape(tile, n, depth, width)
     return estimate * product.transpose(2, 1, 0, 3).reshape(depth, height, width)
 

time: 82 us -> 80.7 us (0.984)
  no operation moved by 1% of the time
where the time goes in v4:
time: 80.7 us; the launch traced here: 80.5 us
  Pallas kernels  76.6 us (95%)
  local copies, waits for them, and re-layouts  3.57 us (4%)
    pallas_call x1, Pallas kernels, local(): pl.pallas_call(functools.partial(kernel, n, m, views, taps), out_shape=ja...  76.6 us

profile of v4, /device:TPU:0, one launch (start us, length us, event | category | flops | bytes accessed | tf_op | source)
XLA Modules:
  0.0 80.5 jit_solution(3995036048903632213)
XLA Ops:
  0.0 1.3 %copy.6.refs_1_ = f32[2,3,31]{2,1,0:T(4,128)} copy(f32[2,3,31]{2,0,1:T(2,128)} %param.6) | data formatting | bytes 1488 | tf_op args[2]
  1.3 76.6 %shard_map.46 = f32[4,8,32,128]{3,2,1,0:T(8,128)} custom-call(s32[2,8,8]{2,1,0:T(8,128)} %refs_0_.1, f32[2,3,31]{2,1,0:T(4,128)} %copy.6.refs_1_, f32[32,32,128]{2,1,0:T(8,128)} %refs_2_.1, f32[2,32,32,128]{3,2,1,0:T(8,128)} %refs_3_.1), custom_call_target="tpu_custom_call" | custom-call | tf_op jit(solution)/shard_map/pallas_call | solution.py:426
  77.9 0.0 copy-start
  77.9 1.1 %copy.7 = f32[32,8,4,128]{3,0,2,1:T(8,128)S(1)} copy(f32[32,8,4,128]{3,0,1,2:T(8,128)} %bitcast.3) | data formatting | bytes 1048576 | tf_op jit(solution)/shard_map/transpose | solution.py:436
  79.0 0.0 copy-done
  79.1 0.3 bitcast_multiply_fusion
  79.4 1.1 %copy.9 = f32[32,32,128]{2,1,0:T(8,128)} copy(f32[32,32,128]{2,0,1:T(8,128)S(1)} %bitcast_multiply_fusion) | data formatting | bytes 1048576 | tf_op jit(solution)/shard_map/mul | solution.py:436
Async XLA Ops:
  77.9 1.2 %copy-start = (f32[32,32,128]{2,1,0:T(8,128)S(1)}, f32[32,32,128]{2,1,0:T(8,128)}, u32[]{:S(2)}) copy-start(f32[32,32,128]{2,1,0:T(8,128)} %refs_2_.1) | copy-start | bytes 1572868
